TPU v7x, 128 devices: a whole 4x4x4 slice. The times are simulated.
128 devices in a mesh: group: 8 (over z, core), member: 16 (over x, y).
Axes of the slice: x: 4, y: 4, z: 4, core: 2. Of those that a mesh axis runs over, the one named last changes fastest.
Arguments:
- tokens: bfloat16 [2048, 3584], P(('group', 'member')), may hold values from -6 to 6
- routes: int32 [2048, 8], P(('group', 'member')), may hold values from 0 to 127, all different within a row; in each aligned block of 16 rows (0 to 15, 16 to 31, ...) at most 2 rows name the same one
- affinity: float32 [2048, 8], P(('group', 'member')), may hold values from -8 to 8
- w_gate: bfloat16 [128, 3584, 1024], P(('group', 'member')), may hold values from -0.09375 to 0.09375
- w_up: bfloat16 [128, 3584, 1024], P(('group', 'member')), may hold values from -0.09375 to 0.09375
- w_down: bfloat16 [128, 1024, 3584], P(('group', 'member')), may hold values from -0.1875 to 0.1875
- q_latent: bfloat16 [1024, 64, 512], P(('group', 'member')), may hold values from -6 to 6
- q_rope: bfloat16 [1024, 4096], P(('group', 'member')), may hold values from -60 to 60
- cache_latent: bfloat16 [1024, 256, 512], P(('group', 'member')), may hold values from -6 to 6
- cache_rope: bfloat16 [1024, 64, 256], P(('group', 'member')), may hold values from -6 to 6
- lengths: int32 [1024], P(('group', 'member')), may hold values from 2 to 256, as said below
Outputs:
- moe_out: bfloat16 [2048, 3584], P(('group', 'member'))
- attn_out: bfloat16 [1024, 32768], P(('group', 'member'))
Inputs may be any that keep to these rules, and one draw needn't show every extreme that they name: `routes`: each row names 8 different experts; among the rows of one device no expert is named by more than 2 rows. `lengths`: some sequence fills its whole cache.
All inputs are finite; a program needn't handle non-finite values.
Results may differ from a plain program's by a relative error of at most 0.0058.
Values may be sent and summed in bfloat16 or wider, within the bound.
A program may use at most 128 MiB of HBM per device.

v0:
```python
import jax
import jax.numpy as jnp
from jax import lax
from jax.sharding import PartitionSpec as P

qk_scale = 192.0 ** (-0.5)
route_scale = 2.5


def per_device(
    tokens,
    routes,
    affinity,
    w_gate,
    w_up,
    w_down,
    q_latent,
    q_rope,
    cache_latent,
    cache_rope,
    lengths,
):
    tok_dev, width = tokens.shape
    topk = routes.shape[1]
    groups = lax.axis_size("group")
    members = lax.axis_size("member")
    experts = groups * members
    capacity = max(2, (tok_dev * topk + experts - 1) // experts * 3 // 2)
    pair_count = tok_dev * topk
    sig = jax.nn.sigmoid(affinity)
    weight = route_scale * sig / jnp.sum(sig, axis=1, keepdims=True)
    flat_routes = routes.reshape(-1)
    onehot = (flat_routes[:, None] == jnp.arange(experts, dtype=jnp.int32)[None, :]).astype(
        jnp.int32
    )
    ranks_run = jnp.cumsum(onehot, axis=0) - 1
    slot_of = jnp.sum(ranks_run * onehot, axis=1)
    position = flat_routes * capacity + slot_of
    pair_token = jnp.arange(pair_count, dtype=jnp.int32) // topk
    token_of = jnp.full((experts * capacity,), tok_dev, jnp.int32).at[position].set(pair_token)
    padded = jnp.concatenate([tokens, jnp.zeros((1, width), jnp.bfloat16)], axis=0)
    outgoing = padded[token_of].reshape(experts, capacity, width)
    gate_w = w_gate[0]
    up_w = w_up[0]
    down_w = w_down[0]
    received = lax.all_to_all(
        outgoing, ("group", "member"), split_axis=0, concat_axis=0, tiled=True
    )
    sources = received.shape[0]
    slots = received.shape[1]
    rows = received.reshape(sources * slots, width)
    gate = jnp.dot(rows, gate_w, preferred_element_type=jnp.float32)
    upper = jnp.dot(rows, up_w, preferred_element_type=jnp.float32)
    hidden = (jax.nn.silu(gate) * upper).astype(jnp.bfloat16)
    result = jnp.dot(hidden, down_w, preferred_element_type=jnp.float32).astype(jnp.bfloat16)
    returned = lax.all_to_all(
        result.reshape(sources, slots, width),
        ("group", "member"),
        split_axis=0,
        concat_axis=0,
        tiled=True,
    )
    flat_back = returned.reshape(experts * capacity, width)
    picked = flat_back[position].reshape(tok_dev, topk, width)
    moe_out = jnp.sum(weight[:, :, None] * picked.astype(jnp.float32), axis=1).astype(jnp.bfloat16)
    seq_dev, heads, latent = q_latent.shape
    rope_width = cache_rope.shape[1]
    cache_len = cache_rope.shape[2]
    rotary = q_rope.reshape(seq_dev, heads, rope_width)
    scores = jnp.einsum("shl,scl->shc", q_latent, cache_latent, preferred_element_type=jnp.float32)
    scores = scores + jnp.einsum(
        "shr,src->shc", rotary, cache_rope, preferred_element_type=jnp.float32
    )
    scores = scores * qk_scale
    valid = jnp.arange(cache_len, dtype=jnp.int32)[None, None, :] < lengths[:, None, None]
    scores = jnp.where(valid, scores, -1e30)
    top_score = jnp.max(scores, axis=2, keepdims=True)
    expo = jnp.where(valid, jnp.exp(scores - top_score), 0.0)
    probs = (expo / jnp.sum(expo, axis=2, keepdims=True)).astype(jnp.bfloat16)
    attended = jnp.einsum("shc,scl->shl", probs, cache_latent, preferred_element_type=jnp.float32)
    attn_out = attended.astype(jnp.bfloat16).reshape(seq_dev, heads * latent)
    return (moe_out, attn_out)


def solution(mesh):
    placed = (
        P(("group", "member"), None),
        P(("group", "member"), None),
        P(("group", "member"), None),
        P(("group", "member"), None, None),
        P(("group", "member"), None, None),
        P(("group", "member"), None, None),
        P(("group", "member"), None, None),
        P(("group", "member"), None),
        P(("group", "member"), None, None),
        P(("group", "member"), None, None),
        P(("group", "member")),
    )
    return jax.shard_map(
        per_device,
        mesh=mesh,
        in_specs=placed,
        out_specs=(P(("group", "member"), None), P(("group", "member"), None)),
        check_vma=False,
    )
```

profile of v0, /device:TPU:2, one launch (start us, length us, event | category | flops | bytes accessed | tf_op | source)
XLA Modules:
  0.0 118.9 jit_solution(7238443512291256652)
XLA Ops:
  0.6 0.0 copy-start
  0.6 0.9 copy.18
  1.6 0.7 broadcast_multiply_fusion
  2.2 0.1 eq.15
  2.3 0.1 fusion.27
  2.4 0.2 reduce_window_sum.11
  2.6 0.2 select_reduce_fusion
  2.8 0.1 copy.17
  2.8 0.1 mul.51
  3.0 1.0 scatter_custom_fusion
  4.0 0.9 concatenate.3
  4.9 2.9 %gather_fusion = bf16[256,3584]{1,0:T(8,128)(2,1)} fusion(bf16[17,3584]{1,0:T(8,128)(2,1)S(1)} %concatenate.3, s32[1024]{0:T(1024)S(1)} %pad_clamp_fusion.1), kind=kCustom, calls=%fused_computation | custom fusion | bytes 3671040 | tf_op jit(solution)/shard_map/gather | solution.py:42
  7.8 4.8 %reshape.80 = bf16[128,2,3584]{2,1,0:T(2,128)(2,1)} reshape(bf16[256,3584]{1,0:T(8,128)(2,1)} %gather_fusion) | data formatting | bytes 3670016 | tf_op jit(solution)/shard_map/reshape | solution.py:42
  12.6 37.3 %all_to_all.10 = bf16[128,2,3584]{2,1,0:T(2,128)(2,1)} all-to-all(bf16[128,2,3584]{2,1,0:T(2,128)(2,1)} %reshape.80), channel_id=1, replica_groups=mesh['group'=8,'member'=16] {'group','member'}, dimensions={0} | all-to-all | bytes 3670016 | tf_op jit(solution)/shard_map/all_to_all | solution.py:46
  50.0 5.0 %reshape.81 = bf16[256,3584]{1,0:T(8,128)(2,1)} reshape(bf16[128,2,3584]{2,1,0:T(2,128)(2,1)} %all_to_all.10) | data formatting | bytes 3670016 | tf_op jit(solution)/shard_map/reshape | solution.py:51
  54.9 5.7 %fusion.5 = f32[256,1024]{1,0:T(8,128)S(1)} fusion(bf16[256,3584]{1,0:T(8,128)(2,1)} %reshape.81, bf16[1,3584,1024]{2,1,0:T(8,128)(2,1)} %param.14), kind=kOutput, calls=%fused_computation.8 | convolution fusion | flops 1879048192 | bytes 10223616 | tf_op jit(solution)/shard_map/dot_general | solution.py:52
  60.6 11.0 %fusion.7 = bf16[256,3584]{1,0:T(8,128)(2,1)} fusion(bf16[1,1024,3584]{2,1,0:T(8,128)(2,1)} %param.16, bf16[256,3584]{1,0:T(8,128)(2,1)} %reshape.81, bf16[1,3584,1024]{2,1,0:T(8,128)(2,1)} %param.15, f32[256,1024]{1,0:T(8,128)S(1)} %fusion.5), kind=kOutput, calls=%fused_computation.10 | convolution fusion | flops 3760586752 | bytes 19398656 | tf_op jit(solution)/shard_map/dot_general | solution.py:55
  71.6 4.8 %reshape.82 = bf16[128,2,3584]{2,1,0:T(2,128)(2,1)} reshape(bf16[256,3584]{1,0:T(8,128)(2,1)} %fusion.7) | data formatting | bytes 3670016 | tf_op jit(solution)/shard_map/reshape | solution.py:57
  76.3 0.0 copy-start.3
  76.3 0.0 copy-start.2
  76.3 0.0 copy-start.4
  76.3 0.0 copy-start.1
  76.3 6.1 %all-to-all-start.1 = ((bf16[128,2,3584]{2,1,0:T(2,128)(2,1)}), bf16[128,2,3584]{2,1,0:T(2,128)(2,1)}, u32[]{:S(2)}, u32[]{:S(2)}) async-start(bf16[128,2,3584]{2,1,0:T(2,128)(2,1)} %reshape.82), calls=%async_computation.1 | async-start | bytes 3670016 | tf_op jit(solution)/shard_map/all_to_all | solution.py:56
  82.4 0.0 copy-done.3
  82.4 0.0 copy-start.5
  82.5 0.1 copy.16
  82.5 0.0 copy-done.2
  82.5 0.2 reshape.84
  82.7 0.0 copy-done.4
  82.7 0.1 iota_compare_fusion.1
  82.8 0.0 copy-done
  82.8 0.0 copy-done.1
  82.8 0.7 fusion.34
  83.6 0.0 copy-done.5
  83.6 1.0 fusion.33
  84.6 1.2 %fusion.20 = bf16[1,8,64,512]{3,2,1,0:T(8,128)(2,1)S(1)} fusion(bf16[8,256,512]{2,1,0:T(8,128)(2,1)S(1)} %copy-done, f32[8,64,256]{2,1,0:T(8,128)S(1)} %get-tuple-element.3, f32[8,64]{1,0:T(8,128)} %get-tuple-element.2), kind=kOutput, calls=%fused_computation.19 | convolution fusion | flops 134742016 | bytes 3147776 | tf_op jit(solution)/shard_map/shc,scl->shl/dot_general | solution.py:80
  85.8 1.1 copy.19
  86.9 22.1 %all-to-all-done.1 = bf16[128,2,3584]{2,1,0:T(2,128)(2,1)} async-done(((bf16[128,2,3584]{2,1,0:T(2,128)(2,1)}), bf16[128,2,3584]{2,1,0:T(2,128)(2,1)}, u32[]{:S(2)}, u32[]{:S(2)}) %all-to-all-start.1) | async-done | bytes 1835040 | tf_op jit(solution)/shard_map/all_to_all | solution.py:56
  108.9 4.9 %reshape.83 = bf16[256,3584]{1,0:T(8,128)(2,1)} reshape(bf16[128,2,3584]{2,1,0:T(2,128)(2,1)} %all-to-all-done.1) | data formatting | bytes 3670016 | tf_op jit(solution)/shard_map/reshape | solution.py:63
  113.8 3.8 %gather_fusion.1 = bf16[128,3584]{1,0:T(8,128)(2,1)S(1)} fusion(bf16[256,3584]{1,0:T(8,128)(2,1)} %reshape.83, s32[1024]{0:T(1024)S(1)} %pad_clamp_fusion), kind=kCustom, calls=%fused_computation.1 | custom fusion | bytes 1835520 | tf_op jit(solution)/shard_map/gather | solution.py:64
  117.6 1.3 %fusion.10 = bf16[16,3584]{1,0:T(8,128)(2,1)} fusion(bf16[128,3584]{1,0:T(8,128)(2,1)S(1)} %gather_fusion.1, f32[16,8]{1,0:T(8,128)S(1)} %copy.16), kind=kLoop, calls=%fused_computation.12 | loop fusion | flops 1318912 | bytes 1032704 | tf_op jit(solution)/shard_map/reduce_sum | solution.py:65
  (7 shorter events, 0.1 us)
Async XLA Ops:
  0.6 82.2 %copy-start = (bf16[8,256,512]{2,1,0:T(8,128)(2,1)S(1)}, bf16[8,256,512]{2,1,0:T(8,128)(2,1)}, u32[]{:S(2)}) copy-start(bf16[8,256,512]{2,1,0:T(8,128)(2,1)} %param.19) | copy-start | bytes 6291460
  76.3 6.1 %copy-start.3 = (f32[16,8]{0,1:T(8,128)S(1)}, f32[16,8]{0,1:T(8,128)}, u32[]{:S(2)}) copy-start(f32[16,8]{0,1:T(8,128)} %param.13) | copy-start | bytes 1540
  76.3 6.2 %copy-start.2 = (bf16[8,4096]{1,0:T(8,128)(2,1)S(1)}, bf16[8,4096]{1,0:T(8,128)(2,1)}, u32[]{:S(2)}) copy-start(bf16[8,4096]{1,0:T(8,128)(2,1)} %param.18) | copy-start | bytes 196612
  76.3 6.4 %copy-start.4 = (s32[8]{0:T(128)S(1)}, s32[8]{0:T(128)}, u32[]{:S(2)}) copy-start(s32[8]{0:T(128)} %param.21) | copy-start | bytes 100
  76.3 6.5 %copy-start.1 = (bf16[8,64,512]{2,1,0:T(8,128)(2,1)S(1)}, bf16[8,64,512]{2,1,0:T(8,128)(2,1)}, u32[]{:S(2)}) copy-start(bf16[8,64,512]{2,1,0:T(8,128)(2,1)} %param.17) | copy-start | bytes 1572868
  76.3 32.6 %all-to-all-start.1 = ((bf16[128,2,3584]{2,1,0:T(2,128)(2,1)}), bf16[128,2,3584]{2,1,0:T(2,128)(2,1)}, u32[]{:S(2)}, u32[]{:S(2)}) async-start(bf16[128,2,3584]{2,1,0:T(2,128)(2,1)} %reshape.82), calls=%async_computation.1 | async-start | bytes 3670016 | tf_op jit(solution)/shard_map/all_to_all | solution.py:56
  82.4 1.2 copy-start.5
where the time goes:
time: 121 us; the launch traced here: 119 us
  blocking collectives  37.3 us (31%)
  local copies, waits for them, and re-layouts  30.5 us (25%)
  waiting for transfers between devices  22.1 us (18%)
  matrix products  19.6 us (16%)
  starting transfers between devices  6.05 us (5%)
  other arithmetic  2.6 us (2%)
    all_to_all x1, blocking collectives, per_device(): lax.all_to_all(outgoing, ('group', 'member'), split_axis=0, concat_axis=0...  37.3 us
    all_to_all x1, waiting for transfers between devices, per_device(): lax.all_to_all(result.reshape(sources, slots, width), ('group', 'member')...  22.1 us
    dot_general x1, matrix products, per_device(): jnp.dot(hidden, down_w, preferred_element_type=jnp.float32)  11 us
    all_to_all x1, starting transfers between devices, per_device(): lax.all_to_all(result.reshape(sources, slots, width), ('group', 'member')...  6.05 us
    dot_general x1, matrix products, per_device(): gate = jnp.dot(rows, gate_w, preferred_element_type=jnp.float32)  5.7 us
    reshape x1, local copies, waits for them, and re-layouts, per_device(): rows = received.reshape(sources * slots, width)  4.95 us
    reshape x1, local copies, waits for them, and re-layouts, per_device(): flat_back = returned.reshape(experts * capacity, width)  4.91 us
    reshape x1, local copies, waits for them, and re-layouts, per_device(): outgoing = padded[token_of].reshape(experts, capacity, width)  4.79 us
  transfers between devices with their start and end apart: 1, of which 1 were waited for; matrix products, arithmetic and copies ran while one was open for 4% of the time, Pallas kernels for 0%

commit v1 on v0

v1 whole, which is shorter than its diff:
```python
import functools

import jax
import jax.numpy as jnp
from jax import lax
from jax.experimental import pallas as pl
from jax.experimental.pallas import tpu as pltpu
from jax.sharding import PartitionSpec as P

MESH = pl.DeviceIdType.MESH
F32 = jnp.float32
BF16 = jnp.bfloat16

ROTATIONS = (("z", "x", "y"), ("x", "y", "z"), ("y", "z", "x"))
TILES = ((5, 5, 4), (4, 5, 5))
LANE = 128
SIDE = 4
TOK = 16
SLOTS = 2
LINE = 2 * SIDE
SOURCES = SIDE * SIDE
HELD = SOURCES * TOK
BLOCK = SOURCES * SLOTS
ROWS = LINE * BLOCK
qk_scale = 192.0 ** (-0.5)
route_scale = 2.5


def columns():
    table, start = [], 0
    for chunk in TILES:
        row = []
        for tiles in chunk:
            row.append((start * LANE, tiles * LANE))
            start += tiles
        table.append(row)
    return table


COLS = columns()
CHUNKS = len(TILES)
PARTS = [(c, r) for c in range(CHUNKS) for r in range(3)]


def dot(a, b):
    return jnp.dot(a, b, preferred_element_type=F32)


def dot_nt(a, b):
    return lax.dot_general(a, b, (((1,), (1,)), ((), ())), preferred_element_type=F32)


def rows_at(index, size):
    return pl.ds(pl.multiple_of(index * size, size), size)


def iota(shape, dim):
    return lax.broadcasted_iota(jnp.int32, shape, dim)


def order_of(rotation, digits):
    a, b, c = ROTATIONS[rotation]
    return (digits[c] * 2 + digits["core"]) * BLOCK + digits["slot"] * SOURCES + digits[b] * SIDE + digits[a]


def digits_of(rotation, index):
    a, b, c = ROTATIONS[rotation]
    return {
        c: index // (2 * BLOCK),
        "core": (index // BLOCK) % 2,
        "slot": (index // SOURCES) % SLOTS,
        b: (index // SIDE) % SIDE,
        a: index % SIDE,
    }


def kernel(
    tokens, routes, affinity, w_gate, w_up, w_down, q_latent, q_rope, cache_latent, cache_rope, lengths,
    moe_out, attn_out,
    *scratch,
):
    it = iter(scratch)

    def take():
        return [[next(it) for _ in range(3)] for _ in range(CHUNKS)]

    held, send, recv, back, part, sum_b, sum_a = (take() for _ in range(7))
    aligned, gate_acc, up_acc, hidden, hidden_r, weigh, perm = (next(it) for _ in range(7))
    routes_v, affinity_v, gate_v, up_v, down_v = (next(it) for _ in range(5))
    ql_v, qr_v, cl_v, cr_v, len_s, q_heads, att, attn_v, moe_v = (next(it) for _ in range(9))
    send_sem, recv_sem, local_sem, weight_sem = (next(it) for _ in range(4))

    group, member = lax.axis_index("group"), lax.axis_index("member")
    me = {"z": group // 2, "core": group % 2, "x": member // 4, "y": member % 4}

    def device(**other):
        at = dict(me)
        at.update(other)
        return (at["z"] * 2 + at["core"], at["x"] * 4 + at["y"])

    barrier = pltpu.get_barrier_semaphore()
    other_core = 1 - me["core"]
    pl.semaphore_signal(barrier, inc=1, device_id=device(core=other_core), device_id_type=MESH)
    for axis in "zxy":
        for k in (1, 3, 2):
            place = (me[axis] + k) % SIDE
            for core in (me["core"], other_core):
                pl.semaphore_signal(barrier, inc=1, device_id=device(**{axis: place, "core": core}), device_id_type=MESH)

    def own_slot(r):
        a, b, _ = ROTATIONS[r]
        return rows_at(me[b] * SIDE + me[a], TOK)

    local = []

    def bring(src, dst):
        copy = pltpu.make_async_copy(src, dst, local_sem.at[len(local)])
        copy.start()
        local.append(copy)
        return copy

    small = [bring(routes, routes_v), bring(affinity, affinity_v)]
    token_copies = []
    for c, r in PARTS:
        start, width = COLS[c][r]
        token_copies.append(bring(tokens.at[:, pl.ds(start, width)], held[c][r].at[own_slot(r), pl.ds(0, width)]))
    attention_copies = [bring(q_rope, qr_v), bring(q_latent, ql_v), bring(cache_latent, cl_v), bring(cache_rope, cr_v), bring(lengths, len_s)]
    weight_copies = {}
    half = gate_v.shape[0] // CHUNKS
    number = 0
    for c in range(CHUNKS):
        for name, src, dst in (("gate", w_gate, gate_v), ("up", w_up, up_v)):
            copy = pltpu.make_async_copy(src.at[0, pl.ds(c * half, half)], dst.at[pl.ds(c * half, half)], weight_sem.at[number])
            copy.start()
            weight_copies[name, c] = copy
            number += 1
    down_copy = pltpu.make_async_copy(w_down.at[0], down_v, weight_sem.at[number])
    down_copy.start()

    for copy in small:
        copy.wait()
    sig = 1.0 / (1.0 + jnp.exp(-affinity_v[...]))
    weight = route_scale * sig / jnp.sum(sig, axis=1, keepdims=True)
    chosen = routes_v[...]
    lanes = iota((TOK, LANE), 1)
    dense = jnp.zeros((TOK, LANE), F32)
    hit = jnp.zeros((TOK, LANE), F32)
    for j in range(chosen.shape[1]):
        same = chosen[:, j : j + 1] == lanes
        dense = jnp.where(same, weight[:, j : j + 1], dense)
        hit = jnp.where(same, 1.0, hit)
    before = (iota((TOK, TOK), 1) < iota((TOK, TOK), 0)).astype(F32).astype(BF16)
    rank = dot(before, hit.astype(BF16))
    code = jnp.where(rank > 0.5, -dense, dense).astype(BF16)
    for r in range(3):
        held[0][r][own_slot(r), pl.ds(COLS[0][r][1], LANE)] = code

    def remote(src, dst, stage, c, r, to):
        return pltpu.make_async_remote_copy(
            src_ref=src, dst_ref=dst,
            send_sem=send_sem.at[stage, c * 3 + r], recv_sem=recv_sem.at[stage, c * 3 + r],
            device_id=to, device_id_type=MESH,
        )

    def await_bytes(ref, sem, stage, c, r):
        pltpu.make_async_copy(ref, ref, sem.at[stage, c * 3 + r]).wait()

    for copy in token_copies:
        copy.wait()
    pl.semaphore_wait(barrier, 1 + 3 * 3 * 2)

    for c, r in PARTS:
        a = ROTATIONS[r][0]
        block = held[c][r].at[own_slot(r)]
        for k in (1, 3, 2):
            remote(block, block, 0, c, r, device(**{a: (me[a] + k) % SIDE})).start()

    for r in (1, 2):
        here = order_of(r, digits_of(0, iota((ROWS, ROWS), 0)))
        perm[r - 1] = jnp.where(here == iota((ROWS, ROWS), 1), 1.0, 0.0).astype(BF16)

    for c, r in PARTS:
        b = ROTATIONS[r][1]
        await_bytes(held[c][r].at[pl.ds(0, 3 * TOK)], recv_sem, 0, c, r)
        block = held[c][r].at[rows_at(me[b], SIDE * TOK)]
        for k in (1, 3, 2):
            remote(block, block, 1, c, r, device(**{b: (me[b] + k) % SIDE})).start()

    for copy in attention_copies:
        copy.wait()
    seqs, heads, latent = ql_v.shape
    rope = cr_v.shape[1]
    cached = cr_v.shape[2]

    def split_heads(p, _):
        pair = qr_v[:, pl.ds(pl.multiple_of(p * LANE, LANE), LANE)].astype(F32)
        q_heads[pl.ds(2 * p, seqs, stride=heads), :] = pair
        q_heads[pl.ds(2 * p + 1, seqs, stride=heads), :] = pltpu.roll(pair, LANE - rope, 1)
        return 0

    lax.fori_loop(0, heads // 2, split_heads, 0)

    def attend(s, _):
        q_rot = q_heads[rows_at(s, heads), :][:, :rope].astype(BF16)
        keys = cl_v[s]
        scores = (dot_nt(ql_v[s], keys) + dot(q_rot, cr_v[s])) * qk_scale
        valid = iota((heads, cached), 1) < len_s[s]
        scores = jnp.where(valid, scores, -1e30)
        top = jnp.max(scores, axis=1, keepdims=True)
        expo = jnp.where(valid, jnp.exp(scores - top), 0.0)
        probs = (expo / jnp.sum(expo, axis=1, keepdims=True)).astype(BF16)
        mixed = dot(probs, keys)
        for q in range(latent // LANE):
            att[q, rows_at(s, heads), :] = mixed[:, q * LANE : (q + 1) * LANE]
        return 0

    lax.fori_loop(0, seqs, attend, 0)

    def join_heads(h, _):
        for q in range(latent // LANE):
            lane = pl.ds(pl.multiple_of(h * latent + q * LANE, LANE), LANE)
            attn_v[:, lane] = att[q, pl.ds(h, seqs, stride=heads), :].astype(BF16)
        return 0

    lax.fori_loop(0, heads, join_heads, 0)
    attn_copy = pltpu.make_async_copy(attn_v, attn_out, local_sem.at[len(local)])
    attn_copy.start()

    source_row = iota((BLOCK, HELD), 0)
    own_source = (source_row % SOURCES) == (iota((BLOCK, HELD), 1) // TOK)
    slot_sign = jnp.where(source_row < SOURCES, 1.0, -1.0)
    line_order = ((1, 0), (3, 1), (2, 0), (3, 0), (1, 1), (2, 1), (0, 1))

    def own_block(r):
        return rows_at(me[ROTATIONS[r][2]] * 2 + me["core"], BLOCK)

    def line_peer(r, k, flip):
        c_axis = ROTATIONS[r][2]
        place, core = (me[c_axis] + k) % SIDE, (me["core"] + flip) % 2
        return rows_at(place * 2 + core, BLOCK), device(**{c_axis: place, "core": core})

    pick = [None] * 3
    for c, r in PARTS:
        width = COLS[c][r][1]
        await_bytes(held[c][r].at[pl.ds(0, 3 * SIDE * TOK)], recv_sem, 1, c, r)
        if c == 0:
            c_axis = ROTATIONS[r][2]
            peer = iota((LINE, LANE), 0)
            at = dict(me)
            at[c_axis] = peer // 2
            expert = (at["z"] * 2 + peer % 2) * 16 + at["x"] * 4 + at["y"]
            select = jnp.where(expert == iota((LINE, LANE), 1), 1.0, 0.0).astype(BF16)
            codes = dot_nt(select, held[c][r][:, pl.ds(width, LANE)])
            ones, scaled = [], []
            for e in range(LINE):
                signed = codes[e : e + 1, :] * slot_sign
                good = jnp.logical_and(own_source, signed > 0.0)
                ones.append(jnp.where(good, 1.0, 0.0).astype(BF16))
                scaled.append(jnp.where(good, signed, 0.0))
            pick[r] = jnp.concatenate(ones, axis=0)
            weigh[r] = jnp.concatenate(scaled, axis=0).T.astype(BF16)
        send[c][r][...] = dot(pick[r], held[c][r][:, pl.ds(0, width)]).astype(BF16)
        for k, flip in line_order:
            block, to = line_peer(r, k, flip)
            remote(send[c][r].at[block], recv[c][r].at[own_block(r)], 2, c, r, to).start()
        recv[c][r][own_block(r), :] = send[c][r][own_block(r), :]

    ff = gate_v.shape[1]
    step = 256
    for c in range(CHUNKS):
        weight_copies["gate", c].wait()
        weight_copies["up", c].wait()
        for r in range(3):
            start, width = COLS[c][r]
            await_bytes(recv[c][r].at[pl.ds(0, (LINE - 1) * BLOCK)], recv_sem, 2, c, r)
            inside = pl.ds(start - c * half, width)
            if r == 0:
                aligned[:, inside] = recv[c][r][...]
            else:
                aligned[:, inside] = dot(perm[r - 1], recv[c][r][...]).astype(BF16)

        def ff_tile(n, _, c=c):
            tile = pl.ds(pl.multiple_of(n * step, step), step)
            gate = dot(aligned[...], gate_v[pl.ds(c * half, half), tile])
            upper = dot(aligned[...], up_v[pl.ds(c * half, half), tile])
            if c > 0:
                gate = gate + gate_acc[:, tile]
                upper = upper + up_acc[:, tile]
            if c < CHUNKS - 1:
                gate_acc[:, tile] = gate
                up_acc[:, tile] = upper
            else:
                hidden[:, tile] = (gate / (1.0 + jnp.exp(-gate)) * upper).astype(BF16)
            return 0

        lax.fori_loop(0, ff // step, ff_tile, 0)

    for r in (1, 2):
        hidden_r[r - 1] = lax.dot_general(
            perm[r - 1], hidden[...], (((0,), (0,)), ((), ())), preferred_element_type=F32
        ).astype(BF16)
    down_copy.wait()
    for c, r in PARTS:
        start, width = COLS[c][r]
        rows = hidden[...] if r == 0 else hidden_r[r - 1]
        await_bytes(recv[c][r].at[pl.ds(0, (LINE - 1) * BLOCK)], send_sem, 2, c, r)
        send[c][r][...] = dot(rows, down_v[:, pl.ds(start, width)]).astype(BF16)
        for k, flip in line_order:
            block, to = line_peer(r, k, flip)
            remote(send[c][r].at[block], back[c][r].at[own_block(r)], 3, c, r, to).start()
        back[c][r][own_block(r), :] = send[c][r][own_block(r), :]

    for c, r in PARTS:
        b = ROTATIONS[r][1]
        await_bytes(back[c][r].at[pl.ds(0, (LINE - 1) * BLOCK)], recv_sem, 3, c, r)
        part[c][r][...] = dot(weigh[r], back[c][r][...]).astype(BF16)
        own = rows_at(me[b], SIDE * TOK)
        for k in (1, 3, 2):
            place = (me[b] + k) % SIDE
            remote(part[c][r].at[rows_at(place, SIDE * TOK)], sum_b[c][r].at[own], 4, c, r, device(**{b: place})).start()
        sum_b[c][r][own, :] = part[c][r][own, :]
    for c, r in PARTS:
        a, b, _ = ROTATIONS[r]
        size = SIDE * TOK
        await_bytes(sum_b[c][r].at[pl.ds(0, 3 * size)], recv_sem, 4, c, r)
        total = sum_b[c][r][pl.ds(0, size), :].astype(F32)
        for k in range(1, SIDE):
            total = total + sum_b[c][r][pl.ds(k * size, size), :].astype(F32)
        await_bytes(part[c][r].at[pl.ds(0, 3 * size)], send_sem, 4, c, r)
        part[c][r][pl.ds(0, size), :] = total.astype(BF16)
        own = rows_at(me[a], TOK)
        for k in (1, 3, 2):
            place = (me[a] + k) % SIDE
            remote(part[c][r].at[rows_at(place, TOK)], sum_a[c][r].at[own], 5, c, r, device(**{a: place})).start()
        sum_a[c][r][own, :] = part[c][r][own, :]
    for c, r in PARTS:
        start, width = COLS[c][r]
        await_bytes(sum_a[c][r].at[pl.ds(0, 3 * TOK)], recv_sem, 5, c, r)
        total = sum_a[c][r][pl.ds(0, TOK), :].astype(F32)
        for k in range(1, SIDE):
            total = total + sum_a[c][r][pl.ds(k * TOK, TOK), :].astype(F32)
        moe_v[:, pl.ds(start, width)] = total.astype(BF16)
    moe_copy = pltpu.make_async_copy(moe_v, moe_out, local_sem.at[len(local) + 1])
    moe_copy.start()

    for c, r in PARTS:
        await_bytes(held[c][r].at[pl.ds(0, 3 * TOK)], send_sem, 0, c, r)
        await_bytes(held[c][r].at[pl.ds(0, 3 * SIDE * TOK)], send_sem, 1, c, r)
        await_bytes(recv[c][r].at[pl.ds(0, (LINE - 1) * BLOCK)], send_sem, 3, c, r)
        await_bytes(sum_a[c][r].at[pl.ds(0, 3 * TOK)], send_sem, 5, c, r)
    attn_copy.wait()
    moe_copy.wait()


def per_device(tokens, routes, affinity, w_gate, w_up, w_down, q_latent, q_rope, cache_latent, cache_rope, lengths):
    tok_dev, width = tokens.shape
    ff = w_gate.shape[2]
    seqs, heads, latent = q_latent.shape
    half = width // CHUNKS

    def buffers(rows, extra=0):
        return [
            pltpu.VMEM((rows, COLS[c][r][1] + (extra if c == 0 else 0)), BF16) for c, r in PARTS
        ]

    scratch = (
        buffers(HELD, LANE)
        + buffers(ROWS) * 3
        + buffers(HELD) * 2
        + buffers(SIDE * TOK)
        + [
            pltpu.VMEM((ROWS, half), BF16),
            pltpu.VMEM((ROWS, ff), F32),
            pltpu.VMEM((ROWS, ff), F32),
            pltpu.VMEM((ROWS, ff), BF16),
            pltpu.VMEM((2, ROWS, ff), BF16),
            pltpu.VMEM((3, HELD, ROWS), BF16),
            pltpu.VMEM((2, ROWS, ROWS), BF16),
            pltpu.VMEM(routes.shape, jnp.int32),
            pltpu.VMEM(affinity.shape, F32),
            pltpu.VMEM((width, ff), BF16),
            pltpu.VMEM((width, ff), BF16),
            pltpu.VMEM((ff, width), BF16),
            pltpu.VMEM(q_latent.shape, BF16),
            pltpu.VMEM(q_rope.shape, BF16),
            pltpu.VMEM(cache_latent.shape, BF16),
            pltpu.VMEM(cache_rope.shape, BF16),
            pltpu.SMEM(lengths.shape, jnp.int32),
            pltpu.VMEM((seqs * heads, LANE), F32),
            pltpu.VMEM((latent // LANE, seqs * heads, LANE), F32),
            pltpu.VMEM((seqs, heads * latent), BF16),
            pltpu.VMEM((tok_dev, width), BF16),
            pltpu.SemaphoreType.DMA((6, len(PARTS))),
            pltpu.SemaphoreType.DMA((6, len(PARTS))),
            pltpu.SemaphoreType.DMA((2 + len(PARTS) + 5 + 2,)),
            pltpu.SemaphoreType.DMA((2 * CHUNKS + 1,)),
        ]
    )
    return pl.pallas_call(
        kernel,
        out_shape=(
            jax.ShapeDtypeStruct((tok_dev, width), BF16),
            jax.ShapeDtypeStruct((seqs, heads * latent), BF16),
        ),
        in_specs=[pl.BlockSpec(memory_space=pl.ANY)] * 11,
        out_specs=[pl.BlockSpec(memory_space=pl.ANY)] * 2,
        scratch_shapes=scratch,
        compiler_params=pltpu.CompilerParams(
            collective_id=0, has_side_effects=True, vmem_limit_bytes=62 * 1024 * 1024
        ),
    )(tokens, routes, affinity, w_gate, w_up, w_down, q_latent, q_rope, cache_latent, cache_rope, lengths)


def solution(mesh):
    rows = P(("group", "member"), None)
    cube = P(("group", "member"), None, None)
    return jax.shard_map(
        per_device,
        mesh=mesh,
        in_specs=(rows, rows, rows, cube, cube, cube, cube, rows, cube, cube, P(("group", "member"))),
        out_specs=(rows, rows),
        check_vma=False,
    )
```

time: 121 us -> 64.9 us (0.54)
  Pallas kernels: 0 us -> 57 us
  blocking collectives: 37.3 us -> 0 us
  local copies, waits for them, and re-layouts: 30.5 us -> 6.13 us
  waiting for transfers between devices: 22.1 us -> 0 us
  matrix products: 19.6 us -> 0 us
  starting transfers between devices: 6.05 us -> 0 us
  other arithmetic: 2.6 us -> 0 us
    pallas_call x0 -> x1, Pallas kernels: none -> 57 us  [per_device(): pl.pallas_call(kernel, out_shape=(jax.ShapeDtypeStruct((tok_dev, width),...]
    all_to_all x1 -> x0, blocking collectives: 37.3 us -> none  [per_device(): lax.all_to_all(outgoing, ('group', 'member'), split_axis=0, concat_axis=0...]
    all_to_all x1 -> x0, waiting for transfers between devices: 22.1 us -> none  [per_device(): lax.all_to_all(result.reshape(sources, slots, width), ('group', 'member')...]
    reshape x5 -> x0, local copies, waits for them, and re-layouts: 19.6 us -> none  [the longest x1 4.95 us: per_device(): rows = received.reshape(sources * slots, width)]
    dot_general x4 -> x0, matrix products: 18.6 us -> none  [the longest x1 11 us: per_device(): jnp.dot(hidden, down_w, preferred_element_type=jnp.float32)]
    gather x2 -> x0, local copies, waits for them, and re-layouts: 6.71 us -> none  [the longest x1 3.76 us: per_device(): picked = flat_back[position].reshape(tok_dev, topk, width)]
    all_to_all x1 -> x0, starting transfers between devices: 6.05 us -> none  [per_device(): lax.all_to_all(result.reshape(sources, slots, width), ('group', 'member')...]
    unnamed x14 -> x4, local copies, waits for them, and re-layouts: 2.02 us -> 6.13 us
  transfers between devices with their start and end apart: 1 -> 0, of which waited for: 1 -> 0; matrix products, arithmetic and copies ran while one was open for 4% -> 0% of each run, Pallas kernels for 0% -> 0%
where the time goes in v1:
time: 64.9 us; the launch traced here: 63.8 us
  Pallas kernels  57 us (88%)
  local copies, waits for them, and re-layouts  6.13 us (9%)
    pallas_call x1, Pallas kernels, per_device(): pl.pallas_call(kernel, out_shape=(jax.ShapeDtypeStruct((tok_dev, width),...  57 us
    unnamed x4, local copies, waits for them, and re-layouts  6.13 us

profile of v1, /device:TPU:2, one launch (start us, length us, event | category | flops | bytes accessed | tf_op | source)
XLA Modules:
  0.0 63.8 jit_solution(6543923936328759538)
XLA Ops:
  0.6 1.4 %copy.13.routes = s32[16,8]{1,0:T(8,128)} copy(s32[16,8]{0,1:T(8,128)} %param.12) | data formatting | bytes 1024 | tf_op args[1]
  2.0 1.4 %copy.14.affinity = f32[16,8]{1,0:T(8,128)} copy(f32[16,8]{0,1:T(8,128)} %param.13) | data formatting | bytes 1024 | tf_op args[2]
  3.3 57.0 %shard_map.122 = (bf16[16,3584]{1,0:T(8,128)(2,1)}, bf16[8,32768]{1,0:T(8,128)(2,1)}) custom-call(bf16[16,3584]{1,0:T(8,128)(2,1)} %tokens.1, s32[16,8]{1,0:T(8,128)} %copy.13.routes, f32[16,8]{1,0:T(8,128)} %copy.14.affinity, bf16[1,3584,1024]{2,1,0:T(8,128)(2,1)} %w_gate.1, bf16[1,3584,1024]{2,1,0:T(8,128)(2,1)} %w_up.1, bf16[1,1024,3584]{2,1,0:T(8,128)(2,1)} %w_down.1, ...), custom_call_target="tpu_custom_call" | custom-call | tf_op jit(solution)/shard_map/pallas_call | solution.py:399
  60.3 1.6 %copy.17 = bf16[16,3584]{1,0:T(8,128)(2,1)} copy(bf16[16,3584]{1,0:T(8,128)(2,1)} %get-tuple-element.4) | data formatting | bytes 229376
  61.9 1.9 %copy.18 = bf16[8,32768]{1,0:T(8,128)(2,1)} copy(bf16[8,32768]{1,0:T(8,128)(2,1)} %get-tuple-element.5) | data formatting | bytes 1048576

commit v2 on v1

v2 whole, which is shorter than its diff:
```python
import functools

import jax
import jax.numpy as jnp
from jax import lax
from jax.experimental import pallas as pl
from jax.experimental.pallas import tpu as pltpu
from jax.sharding import PartitionSpec as P

MESH = pl.DeviceIdType.MESH
F32 = jnp.float32
BF16 = jnp.bfloat16

ROTATIONS = (("z", "x", "y"), ("x", "y", "z"), ("y", "z", "x"))
TILES = ((9, 10, 9),)
LANE = 128
SIDE = 4
TOK = 16
SLOTS = 2
LINE = 2 * SIDE
SOURCES = SIDE * SIDE
WAVES = 2
FEW = SOURCES // WAVES
HELD = FEW * TOK
BLOCK = FEW * SLOTS
ROWS = LINE * BLOCK
GATHER_A, GATHER_B, TO_EXPERT, FROM_EXPERT, SUM_B, SUM_A = range(6)
STAGES = 6
ATTEND = (4, 4)
qk_scale = 192.0 ** (-0.5)
route_scale = 2.5


def columns():
    table, start = [], 0
    for chunk in TILES:
        row = []
        for tiles in chunk:
            row.append((start * LANE, tiles * LANE))
            start += tiles
        table.append(row)
    return table


COLS = columns()
CHUNKS = len(TILES)
PARTS = [(c, r) for c in range(CHUNKS) for r in range(3)]


def dot(a, b):
    return jnp.dot(a, b, preferred_element_type=F32)


def dot_nt(a, b):
    return lax.dot_general(a, b, (((1,), (1,)), ((), ())), preferred_element_type=F32)


def rows_at(index, size):
    return pl.ds(pl.multiple_of(index * size, size), size)


def iota(shape, dim):
    return lax.broadcasted_iota(jnp.int32, shape, dim)


def order_of(rotation, digits):
    a, b, c = ROTATIONS[rotation]
    place = digits[b] * (SIDE // 2) + digits[a] // 2
    return (digits[c] * 2 + digits["core"]) * BLOCK + digits["slot"] * FEW + place


def digits_of(rotation, wave, index):
    a, b, c = ROTATIONS[rotation]
    found = {
        c: index // (2 * BLOCK),
        "core": (index // BLOCK) % 2,
        "slot": (index // FEW) % SLOTS,
        b: (index // 2) % SIDE,
    }
    found[a] = 2 * (index % 2) + (found[b] + found[c] + wave) % 2
    return found


def kernel(
    tokens, routes, affinity, w_gate, w_up, w_down, q_latent, q_rope, cache_latent, cache_rope, lengths,
    moe_out, attn_out,
    *scratch,
):
    it = iter(scratch)

    def take():
        return [[next(it) for _ in range(3)] for _ in range(CHUNKS)]

    held = take()
    send, recv, back, part, sum_b = ([take() for _ in range(WAVES)] for _ in range(5))
    sum_a = take()
    aligned, hidden, hidden_r, weigh, perm = (next(it) for _ in range(5))
    routes_v, affinity_v, gate_v, up_v, down_v = (next(it) for _ in range(5))
    ql_v, qr_v, cl_v, cr_v, len_s, q_heads, att, attn_v, moe_v = (next(it) for _ in range(9))
    send_sem, recv_sem, local_sem, weight_sem = (next(it) for _ in range(4))

    group, member = lax.axis_index("group"), lax.axis_index("member")
    me = {"z": group // 2, "core": group % 2, "x": member // 4, "y": member % 4}

    def device(**other):
        at = dict(me)
        at.update(other)
        return (at["z"] * 2 + at["core"], at["x"] * 4 + at["y"])

    barrier = pltpu.get_barrier_semaphore()
    other_core = 1 - me["core"]
    pl.semaphore_signal(barrier, inc=1, device_id=device(core=other_core), device_id_type=MESH)
    for axis in "zxy":
        for k in (1, 3, 2):
            place = (me[axis] + k) % SIDE
            for core in (me["core"], other_core):
                pl.semaphore_signal(barrier, inc=1, device_id=device(**{axis: place, "core": core}), device_id_type=MESH)

    parity = (me["x"] + me["y"] + me["z"]) % 2

    def slot_of(r, a_place):
        return rows_at(me[ROTATIONS[r][1]] * 2 + a_place // 2, TOK)

    def own_slot(r):
        return slot_of(r, me[ROTATIONS[r][0]])

    local = []

    def bring(src, dst):
        copy = pltpu.make_async_copy(src, dst, local_sem.at[len(local)])
        copy.start()
        local.append(copy)
        return copy

    small = [bring(routes, routes_v), bring(affinity, affinity_v)]
    token_copies = []
    for c, r in PARTS:
        start, width = COLS[c][r]
        token_copies.append(bring(tokens.at[:, pl.ds(start, width)], held[c][r].at[parity, own_slot(r), pl.ds(0, width)]))
    attention_copies = [bring(q_rope, qr_v), bring(q_latent, ql_v), bring(cache_latent, cl_v), bring(cache_rope, cr_v), bring(lengths, len_s)]
    weight_copies = []
    for number, (src, dst) in enumerate(((w_gate, gate_v), (w_up, up_v), (w_down, down_v))):
        weight_copies.append(pltpu.make_async_copy(src.at[0], dst, weight_sem.at[number]))

    for copy in small:
        copy.wait()
    sig = 1.0 / (1.0 + jnp.exp(-affinity_v[...]))
    weight = route_scale * sig / jnp.sum(sig, axis=0, keepdims=True)
    chosen = routes_v[...]
    expert_row = iota((LANE, TOK), 0)
    dense = jnp.zeros((LANE, TOK), F32)
    hit = jnp.zeros((LANE, TOK), F32)
    for j in range(chosen.shape[0]):
        same = chosen[j : j + 1, :] == expert_row
        dense = jnp.where(same, weight[j : j + 1, :], dense)
        hit = jnp.where(same, 1.0, hit)
    before = jnp.where(iota((TOK, TOK), 0) < iota((TOK, TOK), 1), 1.0, 0.0).astype(BF16)
    rank = dot(hit.astype(BF16), before)
    signed = jnp.where(rank > 0.5, -dense, dense)
    code = jnp.concatenate([signed, jnp.zeros((LANE, LANE - TOK), F32)], axis=1).T[:TOK].astype(BF16)
    for r in range(3):
        held[0][r][parity, own_slot(r), pl.ds(COLS[0][r][1], LANE)] = code

    def remote(src, dst, stage, wave, c, r, to):
        part_of = c * 3 + r
        return pltpu.make_async_remote_copy(
            src_ref=src, dst_ref=dst,
            send_sem=send_sem.at[stage, wave, part_of], recv_sem=recv_sem.at[stage, wave, part_of],
            device_id=to, device_id_type=MESH,
        )

    def await_rows(ref, rows, sem, stage, wave, c, r):
        some = ref.at[pl.ds(0, rows)]
        pltpu.make_async_copy(some, some, sem.at[stage, wave, c * 3 + r]).wait()

    for copy in token_copies:
        copy.wait()
    seqs, heads, latent = ql_v.shape
    rope = cr_v.shape[1]
    cached = cr_v.shape[2]

    def split_heads(p, _):
        pair = qr_v[:, pl.ds(pl.multiple_of(p * LANE, LANE), LANE)].astype(F32)
        q_heads[pl.ds(2 * p, seqs, stride=heads), :] = pair
        q_heads[pl.ds(2 * p + 1, seqs, stride=heads), :] = pltpu.roll(pair, LANE - rope, 1)
        return 0

    def attend(s, _):
        q_rot = q_heads[rows_at(s, heads), :][:, :rope].astype(BF16)
        keys = cl_v[s]
        scores = (dot_nt(ql_v[s], keys) + dot(q_rot, cr_v[s])) * qk_scale
        valid = iota((heads, cached), 1) < len_s[s]
        scores = jnp.where(valid, scores, -1e30)
        top = jnp.max(scores, axis=1, keepdims=True)
        expo = jnp.where(valid, jnp.exp(scores - top), 0.0)
        probs = (expo / jnp.sum(expo, axis=1, keepdims=True)).astype(BF16)
        mixed = dot(probs, keys)
        for q in range(latent // LANE):
            att[q, rows_at(s, heads), :] = mixed[:, q * LANE : (q + 1) * LANE]
        return 0

    def join_heads(h, _):
        for q in range(latent // LANE):
            lane = pl.ds(pl.multiple_of(h * latent + q * LANE, LANE), LANE)
            attn_v[:, lane] = att[q, pl.ds(h, seqs, stride=heads), :].astype(BF16)
        return 0

    pl.semaphore_wait(barrier, 1 + 3 * 3 * 2)

    for stage, axis in ((GATHER_A, 0), (GATHER_B, 1)):
        for c, r in PARTS:
            along = ROTATIONS[r][axis]
            block = held[c][r].at[parity, own_slot(r)]
            for k in (1, 3, 2):
                remote(block, block, stage, parity, c, r, device(**{along: (me[along] + k) % SIDE})).start()

    for copy in attention_copies:
        copy.wait()
    for copy in weight_copies:
        copy.start()

    for wave in range(WAVES):
        for r in (1, 2):
            here = order_of(r, digits_of(0, wave, iota((ROWS, ROWS), 0)))
            perm[wave, r - 1] = jnp.where(here == iota((ROWS, ROWS), 1), 1.0, 0.0).astype(BF16)

    lax.fori_loop(0, heads // 2, split_heads, 0, unroll=8)
    lax.fori_loop(0, ATTEND[0], attend, 0, unroll=4)

    for wave in range(WAVES):
        for c, r in PARTS:
            a, b, _ = ROTATIONS[r]
            mine = held[c][r].at[wave]
            far = mine.at[slot_of(r, (me[a] + 2) % SIDE)]
            both = mine.at[rows_at(me[b], 2 * TOK)]

            @pl.when(parity == wave)
            def _():
                await_rows(mine, TOK, recv_sem, GATHER_A, wave, c, r)
                for k in (1, 3, 2):
                    remote(far, far, GATHER_B, wave, c, r, device(**{b: (me[b] + k) % SIDE})).start()

            @pl.when(parity != wave)
            def _():
                await_rows(mine, 2 * TOK, recv_sem, GATHER_A, wave, c, r)
                for k in (1, 3, 2):
                    remote(both, both, GATHER_B, wave, c, r, device(**{b: (me[b] + k) % SIDE})).start()

        if wave == 0:
            lax.fori_loop(ATTEND[0], seqs, attend, 0, unroll=ATTEND[1])
            lax.fori_loop(0, heads, join_heads, 0, unroll=8)
            attn_copy = pltpu.make_async_copy(attn_v, attn_out, local_sem.at[len(local)])
            attn_copy.start()

    place = iota((BLOCK, HELD), 0)
    own_source = place % FEW == iota((BLOCK, HELD), 1) // TOK
    slot_sign = jnp.where(place < FEW, 1.0, -1.0)
    line_order = ((1, 0), (3, 1), (2, 0), (3, 0), (1, 1), (2, 1), (0, 1))

    def own_block(r):
        return rows_at(me[ROTATIONS[r][2]] * 2 + me["core"], BLOCK)

    def line_peer(r, k, flip):
        c_axis = ROTATIONS[r][2]
        at, core = (me[c_axis] + k) % SIDE, (me["core"] + flip) % 2
        return rows_at(at * 2 + core, BLOCK), device(**{c_axis: at, "core": core})

    def exchange(outgoing, incoming, stage, wave, c, r):
        for k, flip in line_order:
            block, to = line_peer(r, k, flip)
            remote(outgoing.at[block], incoming.at[own_block(r)], stage, wave, c, r, to).start()
        incoming[own_block(r), :] = outgoing[own_block(r), :]

    for wave in range(WAVES):
        pick = {}
        for c, r in PARTS:
            width = COLS[c][r][1]
            await_rows(held[c][r].at[wave], 6 * TOK, recv_sem, GATHER_B, wave, c, r)
            if c == 0:
                c_axis = ROTATIONS[r][2]
                peer = iota((LINE, LANE), 0)
                at = dict(me)
                at[c_axis] = peer // 2
                expert = (at["z"] * 2 + peer % 2) * 16 + at["x"] * 4 + at["y"]
                select = jnp.where(expert == iota((LINE, LANE), 1), 1.0, 0.0).astype(BF16)
                codes = dot_nt(select, held[c][r][wave, :, pl.ds(width, LANE)])
                ones, scaled = [], []
                for e in range(LINE):
                    signed = codes[e : e + 1, :] * slot_sign
                    good = jnp.logical_and(own_source, signed > 0.0)
                    ones.append(jnp.where(good, 1.0, 0.0).astype(BF16))
                    scaled.append(jnp.where(good, signed, 0.0))
                pick[r] = jnp.concatenate(ones, axis=0)
                weigh[wave, r] = jnp.concatenate(scaled, axis=0).T.astype(BF16)
            send[wave][c][r][...] = dot(pick[r], held[c][r][wave, :, pl.ds(0, width)]).astype(BF16)
            exchange(send[wave][c][r], recv[wave][c][r], TO_EXPERT, wave, c, r)

    ff = gate_v.shape[1]
    step = 512
    for wave in range(WAVES):
        for c, r in PARTS:
            start, width = COLS[c][r]
            await_rows(recv[wave][c][r], ROWS - BLOCK, recv_sem, TO_EXPERT, wave, c, r)
            if r == 0:
                aligned[:, pl.ds(start, width)] = recv[wave][c][r][...]
            else:
                aligned[:, pl.ds(start, width)] = dot(perm[wave, r - 1], recv[wave][c][r][...]).astype(BF16)
        if wave == 0:
            for copy in weight_copies:
                copy.wait()

        def ff_tile(n, _):
            tile = pl.ds(pl.multiple_of(n * step, step), step)
            gate = dot(aligned[...], gate_v[:, tile])
            upper = dot(aligned[...], up_v[:, tile])
            hidden[:, tile] = (gate / (1.0 + jnp.exp(-gate)) * upper).astype(BF16)
            return 0

        lax.fori_loop(0, ff // step, ff_tile, 0, unroll=True)
        for r in (1, 2):
            hidden_r[r - 1] = lax.dot_general(
                perm[wave, r - 1], hidden[...], (((0,), (0,)), ((), ())), preferred_element_type=F32
            ).astype(BF16)
        for c, r in PARTS:
            start, width = COLS[c][r]
            rows = hidden[...] if r == 0 else hidden_r[r - 1]
            await_rows(send[wave][c][r], ROWS - BLOCK, send_sem, TO_EXPERT, wave, c, r)
            send[wave][c][r][...] = dot(rows, down_v[:, pl.ds(start, width)]).astype(BF16)
            exchange(send[wave][c][r], back[wave][c][r], FROM_EXPERT, wave, c, r)

    pair = 2 * TOK
    for wave in range(WAVES):
        for c, r in PARTS:
            b = ROTATIONS[r][1]
            await_rows(back[wave][c][r], ROWS - BLOCK, recv_sem, FROM_EXPERT, wave, c, r)
            mine = part[wave][c][r]
            mine[...] = dot(weigh[wave, r], back[wave][c][r][...]).astype(BF16)
            own = rows_at(me[b], pair)
            for k in (1, 3, 2):
                to = (me[b] + k) % SIDE
                remote(mine.at[rows_at(to, pair)], sum_b[wave][c][r].at[own], SUM_B, wave, c, r, device(**{b: to})).start()
            sum_b[wave][c][r][own, :] = mine[own, :]
    for wave in range(WAVES):
        for c, r in PARTS:
            a, b, _ = ROTATIONS[r]
            arrived = sum_b[wave][c][r]
            await_rows(arrived, 3 * pair, recv_sem, SUM_B, wave, c, r)
            total = arrived[pl.ds(0, pair), :].astype(F32)
            for k in range(1, SIDE):
                total = total + arrived[pl.ds(k * pair, pair), :].astype(F32)
            mine = part[wave][c][r]
            await_rows(mine, 3 * pair, send_sem, SUM_B, wave, c, r)
            mine[pl.ds(0, pair), :] = total.astype(BF16)
            own = rows_at(me[a], TOK)

            def give(to, c=c, r=r, wave=wave, mine=mine, own=own, a=a):
                remote(mine.at[rows_at(to // 2, TOK)], sum_a[c][r].at[own], SUM_A, wave, c, r, device(**{a: to})).start()

            @pl.when(parity == wave)
            def _():
                give((me[a] + 2) % SIDE)
                sum_a[c][r][own, :] = mine[rows_at(me[a] // 2, TOK), :]

            @pl.when(parity != wave)
            def _():
                give((me[a] + 1) % SIDE)
                give((me[a] + 3) % SIDE)

    for c, r in PARTS:
        start, width = COLS[c][r]
        await_rows(sum_a[c][r], 3 * TOK, recv_sem, SUM_A, parity, c, r)
        total = sum_a[c][r][pl.ds(0, TOK), :].astype(F32)
        for k in range(1, SIDE):
            total = total + sum_a[c][r][pl.ds(k * TOK, TOK), :].astype(F32)
        moe_v[:, pl.ds(start, width)] = total.astype(BF16)
    moe_copy = pltpu.make_async_copy(moe_v, moe_out, local_sem.at[len(local) + 1])
    moe_copy.start()

    for c, r in PARTS:
        await_rows(held[c][r].at[0], 3 * TOK, send_sem, GATHER_A, parity, c, r)
        for wave in range(WAVES):
            await_rows(back[wave][c][r], ROWS - BLOCK, send_sem, FROM_EXPERT, wave, c, r)
            await_rows(held[c][r].at[wave], 6 * TOK, send_sem, GATHER_B, wave, c, r)

            @pl.when(parity == wave)
            def _():
                await_rows(sum_a[c][r], TOK, send_sem, SUM_A, wave, c, r)

            @pl.when(parity != wave)
            def _():
                await_rows(sum_a[c][r], 2 * TOK, send_sem, SUM_A, wave, c, r)

    attn_copy.wait()
    moe_copy.wait()


def per_device(tokens, routes, affinity, w_gate, w_up, w_down, q_latent, q_rope, cache_latent, cache_rope, lengths):
    tok_dev, width = tokens.shape
    ff = w_gate.shape[2]
    seqs, heads, latent = q_latent.shape

    def buffers(rows):
        return [pltpu.VMEM((rows, COLS[c][r][1]), BF16) for c, r in PARTS]

    scratch = (
        [pltpu.VMEM((WAVES, HELD, COLS[c][r][1] + (LANE if c == 0 else 0)), BF16) for c, r in PARTS]
        + buffers(ROWS) * (3 * WAVES)
        + buffers(HELD) * (2 * WAVES)
        + buffers(SIDE * TOK)
        + [
            pltpu.VMEM((ROWS, width), BF16),
            pltpu.VMEM((ROWS, ff), BF16),
            pltpu.VMEM((2, ROWS, ff), BF16),
            pltpu.VMEM((WAVES, 3, HELD, ROWS), BF16),
            pltpu.VMEM((WAVES, 2, ROWS, ROWS), BF16),
            pltpu.VMEM(routes.shape[::-1], jnp.int32),
            pltpu.VMEM(affinity.shape[::-1], F32),
            pltpu.VMEM((width, ff), BF16),
            pltpu.VMEM((width, ff), BF16),
            pltpu.VMEM((ff, width), BF16),
            pltpu.VMEM(q_latent.shape, BF16),
            pltpu.VMEM(q_rope.shape, BF16),
            pltpu.VMEM(cache_latent.shape, BF16),
            pltpu.VMEM(cache_rope.shape, BF16),
            pltpu.SMEM(lengths.shape, jnp.int32),
            pltpu.VMEM((seqs * heads, LANE), F32),
            pltpu.VMEM((latent // LANE, seqs * heads, LANE), F32),
            pltpu.VMEM((seqs, heads * latent), BF16),
            pltpu.VMEM((tok_dev, width), BF16),
            pltpu.SemaphoreType.DMA((STAGES, WAVES, len(PARTS))),
            pltpu.SemaphoreType.DMA((STAGES, WAVES, len(PARTS))),
            pltpu.SemaphoreType.DMA((2 + len(PARTS) + 5 + 2,)),
            pltpu.SemaphoreType.DMA((3,)),
        ]
    )
    results = pl.pallas_call(
        kernel,
        out_shape=(
            jax.ShapeDtypeStruct((tok_dev, width), BF16),
            jax.ShapeDtypeStruct((seqs, heads * latent), BF16),
        ),
        in_specs=[pl.BlockSpec(memory_space=pl.ANY)] * 11,
        out_specs=[pl.BlockSpec(memory_space=pl.ANY)] * 2,
        scratch_shapes=scratch,
        compiler_params=pltpu.CompilerParams(
            collective_id=0, has_side_effects=True, vmem_limit_bytes=62 * 1024 * 1024
        ),
    )(tokens, routes.T, affinity.T, w_gate, w_up, w_down, q_latent, q_rope, cache_latent, cache_rope, lengths)
    anywhere = [pl.BlockSpec(memory_space=pl.ANY)] * 2
    return pl.pallas_call(
        finish,
        out_shape=tuple(jax.ShapeDtypeStruct(x.shape, x.dtype) for x in results),
        in_specs=anywhere,
        out_specs=anywhere,
        scratch_shapes=[pltpu.VMEM(x.shape, x.dtype) for x in results]
        + [pltpu.SemaphoreType.DMA((3,)), pltpu.SemaphoreType.DMA((3,))],
        compiler_params=pltpu.CompilerParams(vmem_limit_bytes=62 * 1024 * 1024),
    )(*results)


def finish(moe_in, attn_in, moe_out, attn_out, moe_v, attn_v, in_sem, out_sem):
    half = attn_in.shape[1] // 2
    pieces = [(moe_in, moe_v, moe_out)]
    for i in range(2):
        pieces.append(tuple(ref.at[:, pl.ds(i * half, half)] for ref in (attn_in, attn_v, attn_out)))
    first = [pltpu.make_async_copy(src, mid, in_sem.at[i]) for i, (src, mid, _) in enumerate(pieces)]
    last = [pltpu.make_async_copy(mid, dst, out_sem.at[i]) for i, (_, mid, dst) in enumerate(pieces)]
    for copy in first:
        copy.start()
    for copy, then in zip(first, last):
        copy.wait()
        then.start()
    for copy in last:
        copy.wait()


def solution(mesh):
    rows = P(("group", "member"), None)
    cube = P(("group", "member"), None, None)
    return jax.shard_map(
        per_device,
        mesh=mesh,
        in_specs=(rows, rows, rows, cube, cube, cube, cube, rows, cube, cube, P(("group", "member"))),
        out_specs=(rows, rows),
        check_vma=False,
    )
```

time: 64.9 us -> 54 us (0.83); the launches traced: 63.8 us -> 53.9 us
  local copies, waits for them, and re-layouts: 6.13 us -> 0 us
  Pallas kernels: 57 us -> 53.2 us
    unnamed x4 -> x0, local copies, waits for them, and re-layouts: 6.13 us -> none
    pallas_call x1, Pallas kernels: 57 us -> 51.4 us  [per_device(): pl.pallas_call(kernel, out_shape=(jax.ShapeDtypeStruct((tok_dev, width),...]
    pallas_call x0 -> x1, Pallas kernels: none -> 1.85 us  [per_device(): pl.pallas_call(finish, out_shape=tuple((jax.ShapeDtypeStruct(x.shape, x.d...]
where the time goes in v2:
time: 54 us; the launch traced here: 53.9 us
  Pallas kernels  53.2 us (99%)
  between operations  0.64 us (1%)
    pallas_call x1, Pallas kernels, per_device(): pl.pallas_call(kernel, out_shape=(jax.ShapeDtypeStruct((tok_dev, width),...  51.4 us
    pallas_call x1, Pallas kernels, per_device(): pl.pallas_call(finish, out_shape=tuple((jax.ShapeDtypeStruct(x.shape, x.d...  1.85 us

profile of v2, /device:TPU:2, one launch (start us, length us, event | category | flops | bytes accessed | tf_op | source)
XLA Modules:
  0.0 53.9 jit_solution(8241429096648526795)
XLA Ops:
  0.6 51.4 %shard_map.122 = (bf16[16,3584]{1,0:T(8,128)(2,1)}, bf16[8,32768]{1,0:T(8,128)(2,1)}) custom-call(bf16[16,3584]{1,0:T(8,128)(2,1)} %tokens.1, s32[8,16]{1,0:T(8,128)} %bitcast.2, f32[8,16]{1,0:T(8,128)} %bitcast.3, bf16[1,3584,1024]{2,1,0:T(8,128)(2,1)} %w_gate.1, bf16[1,3584,1024]{2,1,0:T(8,128)(2,1)} %w_up.1, bf16[1,1024,3584]{2,1,0:T(8,128)(2,1)} %w_down.1, ...), custom_call_target="tpu_custom_call" | custom-call | tf_op jit(solution)/shard_map/pallas_call | solution.py:436
  52.0 1.9 %shard_map.123 = (bf16[16,3584]{1,0:T(8,128)(2,1)}, bf16[8,32768]{1,0:T(8,128)(2,1)}) custom-call(bf16[16,3584]{1,0:T(8,128)(2,1)} %get-tuple-element.4.moe_in, bf16[8,32768]{1,0:T(8,128)(2,1)} %get-tuple-element.5.attn_in), custom_call_target="tpu_custom_call" | custom-call | tf_op jit(solution)/shard_map/pallas_call | solution.py:450

commit v3 on v2

--- a/solution.py
+++ b/solution.py
@@ -24,9 +24,9 @@
 HELD = FEW * TOK
 BLOCK = FEW * SLOTS
 ROWS = LINE * BLOCK
-GATHER_A, GATHER_B, TO_EXPERT, FROM_EXPERT, SUM_B, SUM_A = range(6)
-STAGES = 6
-ATTEND = (4, 4)
+GATHER_A, GATHER_B, TO_EXPERT, FROM_EXPERT, SUM_B, SUM_A, CODE_A, CODE_B = range(8)
+STAGES = 8
+ATTEND = (2, 2, 2)
 qk_scale = 192.0 ** (-0.5)
 route_scale = 2.5
 
@@ -92,8 +92,9 @@
         return [[next(it) for _ in range(3)] for _ in range(CHUNKS)]
 
     held = take()
-    send, recv, back, part, sum_b = ([take() for _ in range(WAVES)] for _ in range(5))
+    send, recv, result, back, part, sum_b, both_b = ([take() for _ in range(WAVES)] for _ in range(7))
     sum_a = take()
+    codes_v = [next(it) for _ in range(3)]
     aligned, hidden, hidden_r, weigh, perm = (next(it) for _ in range(5))
     routes_v, affinity_v, gate_v, up_v, down_v = (next(it) for _ in range(5))
     ql_v, qr_v, cl_v, cr_v, len_s, q_heads, att, attn_v, moe_v = (next(it) for _ in range(9))
@@ -136,11 +137,66 @@
     token_copies = []
     for c, r in PARTS:
         start, width = COLS[c][r]
-        token_copies.append(bring(tokens.at[:, pl.ds(start, width)], held[c][r].at[parity, own_slot(r), pl.ds(0, width)]))
+        token_copies.append(bring(tokens.at[:, pl.ds(start, width)], held[c][r].at[parity, own_slot(r)]))
     attention_copies = [bring(q_rope, qr_v), bring(q_latent, ql_v), bring(cache_latent, cl_v), bring(cache_rope, cr_v), bring(lengths, len_s)]
     weight_copies = []
     for number, (src, dst) in enumerate(((w_gate, gate_v), (w_up, up_v), (w_down, down_v))):
         weight_copies.append(pltpu.make_async_copy(src.at[0], dst, weight_sem.at[number]))
+
+    def remote(src, dst, stage, wave, c, r, to):
+        part_of = c * 3 + r
+        return pltpu.make_async_remote_copy(
+            src_ref=src, dst_ref=dst,
+            send_sem=send_sem.at[stage, wave, part_of], recv_sem=recv_sem.at[stage, wave, part_of],
+            device_id=to, device_id_type=MESH,
+        )
+
+    def await_rows(ref, rows, sem, stage, wave, c, r):
+        some = ref.at[pl.ds(0, rows)]
+        pltpu.make_async_copy(some, some, sem.at[stage, wave, c * 3 + r]).wait()
+
+    for copy in token_copies:
+        copy.wait()
+    seqs, heads, latent = ql_v.shape
+    rope = cr_v.shape[1]
+    cached = cr_v.shape[2]
+
+    def split_heads(p, _):
+        pair = qr_v[:, pl.ds(pl.multiple_of(p * LANE, LANE), LANE)].astype(F32)
+        q_heads[pl.ds(2 * p, seqs, stride=heads), :] = pair
+        q_heads[pl.ds(2 * p + 1, seqs, stride=heads), :] = pltpu.roll(pair, LANE - rope, 1)
+        return 0
+
+    def attend(s, _):
+        q_rot = q_heads[rows_at(s, heads), :][:, :rope].astype(BF16)
+        keys = cl_v[s]
+        scores = (dot_nt(ql_v[s], keys) + dot(q_rot, cr_v[s])) * qk_scale
+        valid = iota((heads, cached), 1) < len_s[s]
+        scores = jnp.where(valid, scores, -1e30)
+        top = jnp.max(scores, axis=1, keepdims=True)
+        expo = jnp.where(valid, jnp.exp(scores - top), 0.0)
+        probs = (expo / jnp.sum(expo, axis=1, keepdims=True)).astype(BF16)
+        mixed = dot(probs, keys)
+        for q in range(latent // LANE):
+            att[q, rows_at(s, heads), :] = mixed[:, q * LANE : (q + 1) * LANE]
+        return 0
+
+    def join_heads(h, _):
+        for q in range(latent // LANE):
+            lane = pl.ds(pl.multiple_of(h * latent + q * LANE, LANE), LANE)
+            attn_v[:, lane] = att[q, pl.ds(h, seqs, stride=heads), :].astype(BF16)
+        return 0
+
+    pl.semaphore_wait(barrier, 1 + 3 * 3 * 2)
+
+    def send_own(stage, axis, refs, c, r):
+        along = ROTATIONS[r][axis]
+        block = refs.at[parity, own_slot(r)]
+        for k in (1, 3, 2):
+            remote(block, block, stage, parity, c, r, device(**{along: (me[along] + k) % SIDE})).start()
+
+    for c, r in PARTS:
+        send_own(GATHER_A, 0, held[c][r], c, r)
 
     for copy in small:
         copy.wait()
@@ -159,98 +215,54 @@
     signed = jnp.where(rank > 0.5, -dense, dense)
     code = jnp.concatenate([signed, jnp.zeros((LANE, LANE - TOK), F32)], axis=1).T[:TOK].astype(BF16)
     for r in range(3):
-        held[0][r][parity, own_slot(r), pl.ds(COLS[0][r][1], LANE)] = code
-
-    def remote(src, dst, stage, wave, c, r, to):
-        part_of = c * 3 + r
-        return pltpu.make_async_remote_copy(
-            src_ref=src, dst_ref=dst,
-            send_sem=send_sem.at[stage, wave, part_of], recv_sem=recv_sem.at[stage, wave, part_of],
-            device_id=to, device_id_type=MESH,
-        )
-
-    def await_rows(ref, rows, sem, stage, wave, c, r):
-        some = ref.at[pl.ds(0, rows)]
-        pltpu.make_async_copy(some, some, sem.at[stage, wave, c * 3 + r]).wait()
-
-    for copy in token_copies:
-        copy.wait()
-    seqs, heads, latent = ql_v.shape
-    rope = cr_v.shape[1]
-    cached = cr_v.shape[2]
-
-    def split_heads(p, _):
-        pair = qr_v[:, pl.ds(pl.multiple_of(p * LANE, LANE), LANE)].astype(F32)
-        q_heads[pl.ds(2 * p, seqs, stride=heads), :] = pair
-        q_heads[pl.ds(2 * p + 1, seqs, stride=heads), :] = pltpu.roll(pair, LANE - rope, 1)
-        return 0
-
-    def attend(s, _):
-        q_rot = q_heads[rows_at(s, heads), :][:, :rope].astype(BF16)
-        keys = cl_v[s]
-        scores = (dot_nt(ql_v[s], keys) + dot(q_rot, cr_v[s])) * qk_scale
-        valid = iota((heads, cached), 1) < len_s[s]
-        scores = jnp.where(valid, scores, -1e30)
-        top = jnp.max(scores, axis=1, keepdims=True)
-        expo = jnp.where(valid, jnp.exp(scores - top), 0.0)
-        probs = (expo / jnp.sum(expo, axis=1, keepdims=True)).astype(BF16)
-        mixed = dot(probs, keys)
-        for q in range(latent // LANE):
-            att[q, rows_at(s, heads), :] = mixed[:, q * LANE : (q + 1) * LANE]
-        return 0
-
-    def join_heads(h, _):
-        for q in range(latent // LANE):
-            lane = pl.ds(pl.multiple_of(h * latent + q * LANE, LANE), LANE)
-            attn_v[:, lane] = att[q, pl.ds(h, seqs, stride=heads), :].astype(BF16)
-        return 0
-
-    pl.semaphore_wait(barrier, 1 + 3 * 3 * 2)
-
-    for stage, axis in ((GATHER_A, 0), (GATHER_B, 1)):
-        for c, r in PARTS:
-            along = ROTATIONS[r][axis]
-            block = held[c][r].at[parity, own_slot(r)]
-            for k in (1, 3, 2):
-                remote(block, block, stage, parity, c, r, device(**{along: (me[along] + k) % SIDE})).start()
-
+        codes_v[r][parity, own_slot(r), :] = code
+
+    for c, r in PARTS:
+        send_own(GATHER_B, 1, held[c][r], c, r)
+    for r in range(3):
+        send_own(CODE_A, 0, codes_v[r], 0, r)
+    for r in range(3):
+        send_own(CODE_B, 1, codes_v[r], 0, r)
     for copy in attention_copies:
         copy.wait()
     for copy in weight_copies:
         copy.start()
+    lax.fori_loop(0, heads // 2, split_heads, 0, unroll=8)
+
+    lax.fori_loop(0, ATTEND[0], attend, 0, unroll=True)
 
     for wave in range(WAVES):
         for r in (1, 2):
             here = order_of(r, digits_of(0, wave, iota((ROWS, ROWS), 0)))
-            perm[wave, r - 1] = jnp.where(here == iota((ROWS, ROWS), 1), 1.0, 0.0).astype(BF16)
-
-    lax.fori_loop(0, heads // 2, split_heads, 0, unroll=8)
-    lax.fori_loop(0, ATTEND[0], attend, 0, unroll=4)
+            perm[wave, :, pl.ds((r - 1) * ROWS, ROWS)] = jnp.where(here == iota((ROWS, ROWS), 1), 1.0, 0.0).astype(BF16)
+
+    lax.fori_loop(ATTEND[0], ATTEND[0] + ATTEND[1], attend, 0, unroll=True)
+
+    def pass_on(refs, stages, wave, c, r):
+        a, b, _ = ROTATIONS[r]
+        mine = refs.at[wave]
+        far = mine.at[slot_of(r, (me[a] + 2) % SIDE)]
+        both = mine.at[rows_at(me[b], 2 * TOK)]
+
+        @pl.when(parity == wave)
+        def _():
+            await_rows(mine, TOK, recv_sem, stages[0], wave, c, r)
+            for k in (1, 3, 2):
+                remote(far, far, stages[1], wave, c, r, device(**{b: (me[b] + k) % SIDE})).start()
+
+        @pl.when(parity != wave)
+        def _():
+            await_rows(mine, 2 * TOK, recv_sem, stages[0], wave, c, r)
+            for k in (1, 3, 2):
+                remote(both, both, stages[1], wave, c, r, device(**{b: (me[b] + k) % SIDE})).start()
 
     for wave in range(WAVES):
         for c, r in PARTS:
-            a, b, _ = ROTATIONS[r]
-            mine = held[c][r].at[wave]
-            far = mine.at[slot_of(r, (me[a] + 2) % SIDE)]
-            both = mine.at[rows_at(me[b], 2 * TOK)]
-
-            @pl.when(parity == wave)
-            def _():
-                await_rows(mine, TOK, recv_sem, GATHER_A, wave, c, r)
-                for k in (1, 3, 2):
-                    remote(far, far, GATHER_B, wave, c, r, device(**{b: (me[b] + k) % SIDE})).start()
-
-            @pl.when(parity != wave)
-            def _():
-                await_rows(mine, 2 * TOK, recv_sem, GATHER_A, wave, c, r)
-                for k in (1, 3, 2):
-                    remote(both, both, GATHER_B, wave, c, r, device(**{b: (me[b] + k) % SIDE})).start()
-
+            pass_on(held[c][r], (GATHER_A, GATHER_B), wave, c, r)
+        for r in range(3):
+            pass_on(codes_v[r], (CODE_A, CODE_B), wave, 0, r)
         if wave == 0:
-            lax.fori_loop(ATTEND[0], seqs, attend, 0, unroll=ATTEND[1])
-            lax.fori_loop(0, heads, join_heads, 0, unroll=8)
-            attn_copy = pltpu.make_async_copy(attn_v, attn_out, local_sem.at[len(local)])
-            attn_copy.start()
+            lax.fori_loop(ATTEND[0] + ATTEND[1], sum(ATTEND), attend, 0, unroll=True)
 
     place = iota((BLOCK, HELD), 0)
     own_source = place % FEW == iota((BLOCK, HELD), 1) // TOK
@@ -271,40 +283,59 @@
             remote(outgoing.at[block], incoming.at[own_block(r)], stage, wave, c, r, to).start()
         incoming[own_block(r), :] = outgoing[own_block(r), :]
 
-    for wave in range(WAVES):
-        pick = {}
-        for c, r in PARTS:
-            width = COLS[c][r][1]
-            await_rows(held[c][r].at[wave], 6 * TOK, recv_sem, GATHER_B, wave, c, r)
-            if c == 0:
-                c_axis = ROTATIONS[r][2]
-                peer = iota((LINE, LANE), 0)
-                at = dict(me)
-                at[c_axis] = peer // 2
-                expert = (at["z"] * 2 + peer % 2) * 16 + at["x"] * 4 + at["y"]
-                select = jnp.where(expert == iota((LINE, LANE), 1), 1.0, 0.0).astype(BF16)
-                codes = dot_nt(select, held[c][r][wave, :, pl.ds(width, LANE)])
-                ones, scaled = [], []
-                for e in range(LINE):
-                    signed = codes[e : e + 1, :] * slot_sign
-                    good = jnp.logical_and(own_source, signed > 0.0)
-                    ones.append(jnp.where(good, 1.0, 0.0).astype(BF16))
-                    scaled.append(jnp.where(good, signed, 0.0))
-                pick[r] = jnp.concatenate(ones, axis=0)
-                weigh[wave, r] = jnp.concatenate(scaled, axis=0).T.astype(BF16)
-            send[wave][c][r][...] = dot(pick[r], held[c][r][wave, :, pl.ds(0, width)]).astype(BF16)
-            exchange(send[wave][c][r], recv[wave][c][r], TO_EXPERT, wave, c, r)
+    scaled = {}
+    for wave in range(WAVES):
+        pick = []
+        for r in range(3):
+            await_rows(codes_v[r].at[wave], 6 * TOK, recv_sem, CODE_B, wave, 0, r)
+            c_axis = ROTATIONS[r][2]
+            peer = iota((LINE, LANE), 0)
+            at = dict(me)
+            at[c_axis] = peer // 2
+            expert = (at["z"] * 2 + peer % 2) * 16 + at["x"] * 4 + at["y"]
+            select = jnp.where(expert == iota((LINE, LANE), 1), 1.0, 0.0).astype(BF16)
+            codes = dot_nt(select, codes_v[r][wave])
+            parts = []
+            for e in range(LINE):
+                signed = codes[e : e + 1, :] * slot_sign
+                parts.append(jnp.where(jnp.logical_and(own_source, signed > 0.0), signed, 0.0))
+            scaled[wave, r] = jnp.concatenate(parts, axis=0)
+            pick.append(jnp.where(scaled[wave, r] > 0.0, 1.0, 0.0).astype(BF16))
+        for c in range(CHUNKS):
+            for r in range(3):
+                await_rows(held[c][r].at[wave], 6 * TOK, recv_sem, GATHER_B, wave, c, r)
+            for r in range(3):
+                send[wave][c][r][...] = dot(pick[r], held[c][r][wave]).astype(BF16)
+            for r in range(3):
+                exchange(send[wave][c][r], recv[wave][c][r], TO_EXPERT, wave, c, r)
+    for wave in range(WAVES):
+        for r in range(3):
+            weigh[wave, r] = scaled[wave, r].T.astype(BF16)
+
+    pair = 2 * TOK
+
+    def combine(wave, c, r):
+        b = ROTATIONS[r][1]
+        await_rows(back[wave][c][r], ROWS - BLOCK, recv_sem, FROM_EXPERT, wave, c, r)
+        mine = part[wave][c][r]
+        mine[...] = dot(weigh[wave, r], back[wave][c][r][...]).astype(BF16)
+        own = rows_at(me[b], pair)
+        for k in (1, 3, 2):
+            to = (me[b] + k) % SIDE
+            remote(mine.at[rows_at(to, pair)], sum_b[wave][c][r].at[own], SUM_B, wave, c, r, device(**{b: to})).start()
+        sum_b[wave][c][r][own, :] = mine[own, :]
 
     ff = gate_v.shape[1]
     step = 512
     for wave in range(WAVES):
         for c, r in PARTS:
+            await_rows(recv[wave][c][r], ROWS - BLOCK, recv_sem, TO_EXPERT, wave, c, r)
+        for c, r in PARTS:
             start, width = COLS[c][r]
-            await_rows(recv[wave][c][r], ROWS - BLOCK, recv_sem, TO_EXPERT, wave, c, r)
             if r == 0:
                 aligned[:, pl.ds(start, width)] = recv[wave][c][r][...]
             else:
-                aligned[:, pl.ds(start, width)] = dot(perm[wave, r - 1], recv[wave][c][r][...]).astype(BF16)
+                aligned[:, pl.ds(start, width)] = dot(perm[wave, :, pl.ds((r - 1) * ROWS, ROWS)], recv[wave][c][r][...]).astype(BF16)
         if wave == 0:
             for copy in weight_copies:
                 copy.wait()
@@ -317,29 +348,23 @@
             return 0
 
         lax.fori_loop(0, ff // step, ff_tile, 0, unroll=True)
-        for r in (1, 2):
-            hidden_r[r - 1] = lax.dot_general(
-                perm[wave, r - 1], hidden[...], (((0,), (0,)), ((), ())), preferred_element_type=F32
-            ).astype(BF16)
+        hidden_r[...] = lax.dot_general(
+            perm[wave], hidden[...], (((0,), (0,)), ((), ())), preferred_element_type=F32
+        ).astype(BF16)
         for c, r in PARTS:
             start, width = COLS[c][r]
-            rows = hidden[...] if r == 0 else hidden_r[r - 1]
-            await_rows(send[wave][c][r], ROWS - BLOCK, send_sem, TO_EXPERT, wave, c, r)
-            send[wave][c][r][...] = dot(rows, down_v[:, pl.ds(start, width)]).astype(BF16)
-            exchange(send[wave][c][r], back[wave][c][r], FROM_EXPERT, wave, c, r)
-
-    pair = 2 * TOK
+            rows = hidden[...] if r == 0 else hidden_r[pl.ds((r - 1) * ROWS, ROWS), :]
+            result[wave][c][r][...] = dot(rows, down_v[:, pl.ds(start, width)]).astype(BF16)
+            exchange(result[wave][c][r], back[wave][c][r], FROM_EXPERT, wave, c, r)
+    lax.fori_loop(sum(ATTEND), seqs, attend, 0, unroll=True)
+    lax.fori_loop(0, heads, join_heads, 0, unroll=8)
+    attn_copy = pltpu.make_async_copy(attn_v, attn_out, local_sem.at[len(local)])
+    attn_copy.start()
+
     for wave in range(WAVES):
         for c, r in PARTS:
-            b = ROTATIONS[r][1]
-            await_rows(back[wave][c][r], ROWS - BLOCK, recv_sem, FROM_EXPERT, wave, c, r)
-            mine = part[wave][c][r]
-            mine[...] = dot(weigh[wave, r], back[wave][c][r][...]).astype(BF16)
-            own = rows_at(me[b], pair)
-            for k in (1, 3, 2):
-                to = (me[b] + k) % SIDE
-                remote(mine.at[rows_at(to, pair)], sum_b[wave][c][r].at[own], SUM_B, wave, c, r, device(**{b: to})).start()
-            sum_b[wave][c][r][own, :] = mine[own, :]
+            combine(wave, c, r)
+
     for wave in range(WAVES):
         for c, r in PARTS:
             a, b, _ = ROTATIONS[r]
@@ -348,9 +373,8 @@
             total = arrived[pl.ds(0, pair), :].astype(F32)
             for k in range(1, SIDE):
                 total = total + arrived[pl.ds(k * pair, pair), :].astype(F32)
-            mine = part[wave][c][r]
-            await_rows(mine, 3 * pair, send_sem, SUM_B, wave, c, r)
-            mine[pl.ds(0, pair), :] = total.astype(BF16)
+            mine = both_b[wave][c][r]
+            mine[...] = total.astype(BF16)
             own = rows_at(me[a], TOK)
 
             def give(to, c=c, r=r, wave=wave, mine=mine, own=own, a=a):
@@ -378,8 +402,14 @@
 
     for c, r in PARTS:
         await_rows(held[c][r].at[0], 3 * TOK, send_sem, GATHER_A, parity, c, r)
+        if c == 0:
+            await_rows(codes_v[r].at[0], 3 * TOK, send_sem, CODE_A, parity, 0, r)
         for wave in range(WAVES):
+            if c == 0:
+                await_rows(codes_v[r].at[wave], 6 * TOK, send_sem, CODE_B, wave, 0, r)
+            await_rows(back[wave][c][r], ROWS - BLOCK, send_sem, TO_EXPERT, wave, c, r)
             await_rows(back[wave][c][r], ROWS - BLOCK, send_sem, FROM_EXPERT, wave, c, r)
+            await_rows(sum_b[wave][c][r], 3 * pair, send_sem, SUM_B, wave, c, r)
             await_rows(held[c][r].at[wave], 6 * TOK, send_sem, GATHER_B, wave, c, r)
 
             @pl.when(parity == wave)
@@ -389,7 +419,6 @@
             @pl.when(parity != wave)
             def _():
                 await_rows(sum_a[c][r], 2 * TOK, send_sem, SUM_A, wave, c, r)
-
     attn_copy.wait()
     moe_copy.wait()
 
@@ -403,16 +432,18 @@
         return [pltpu.VMEM((rows, COLS[c][r][1]), BF16) for c, r in PARTS]
 
     scratch = (
-        [pltpu.VMEM((WAVES, HELD, COLS[c][r][1] + (LANE if c == 0 else 0)), BF16) for c, r in PARTS]
-        + buffers(ROWS) * (3 * WAVES)
+        [pltpu.VMEM((WAVES, HELD, COLS[c][r][1]), BF16) for c, r in PARTS]
+        + buffers(ROWS) * (4 * WAVES)
         + buffers(HELD) * (2 * WAVES)
+        + buffers(2 * TOK) * WAVES
         + buffers(SIDE * TOK)
+        + [pltpu.VMEM((WAVES, HELD, LANE), BF16)] * 3
         + [
             pltpu.VMEM((ROWS, width), BF16),
             pltpu.VMEM((ROWS, ff), BF16),
-            pltpu.VMEM((2, ROWS, ff), BF16),
+            pltpu.VMEM((2 * ROWS, ff), BF16),
             pltpu.VMEM((WAVES, 3, HELD, ROWS), BF16),
-            pltpu.VMEM((WAVES, 2, ROWS, ROWS), BF16),
+            pltpu.VMEM((WAVES, ROWS, 2 * ROWS), BF16),
             pltpu.VMEM(routes.shape[::-1], jnp.int32),
             pltpu.VMEM(affinity.shape[::-1], F32),
             pltpu.VMEM((width, ff), BF16),

time: 54 us -> 53.4 us (0.989)
    pallas_call x1, Pallas kernels: 51.4 us -> 50.8 us  [per_device(): pl.pallas_call(kernel, out_shape=(jax.ShapeDtypeStruct((tok_dev, width),...]
where the time goes in v3:
time: 53.4 us; the launch traced here: 53.3 us
  Pallas kernels  52.7 us (99%)
  between operations  0.64 us (1%)
    pallas_call x1, Pallas kernels, per_device(): pl.pallas_call(kernel, out_shape=(jax.ShapeDtypeStruct((tok_dev, width),...  50.8 us
    pallas_call x1, Pallas kernels, per_device(): pl.pallas_call(finish, out_shape=tuple((jax.ShapeDtypeStruct(x.shape, x.d...  1.85 us

profile of v3, /device:TPU:2, one launch (start us, length us, event | category | flops | bytes accessed | tf_op | source)
XLA Modules:
  0.0 53.3 jit_solution(10874229466365751844)
XLA Ops:
  0.6 50.8 %shard_map.122 = (bf16[16,3584]{1,0:T(8,128)(2,1)}, bf16[8,32768]{1,0:T(8,128)(2,1)}) custom-call(bf16[16,3584]{1,0:T(8,128)(2,1)} %tokens.1, s32[8,16]{1,0:T(8,128)} %bitcast.2, f32[8,16]{1,0:T(8,128)} %bitcast.3, bf16[1,3584,1024]{2,1,0:T(8,128)(2,1)} %w_gate.1, bf16[1,3584,1024]{2,1,0:T(8,128)(2,1)} %w_up.1, bf16[1,1024,3584]{2,1,0:T(8,128)(2,1)} %w_down.1, ...), custom_call_target="tpu_custom_call" | custom-call | tf_op jit(solution)/shard_map/pallas_call | solution.py:467
  51.4 1.9 %shard_map.123 = (bf16[16,3584]{1,0:T(8,128)(2,1)}, bf16[8,32768]{1,0:T(8,128)(2,1)}) custom-call(bf16[16,3584]{1,0:T(8,128)(2,1)} %get-tuple-element.4.moe_in, bf16[8,32768]{1,0:T(8,128)(2,1)} %get-tuple-element.5.attn_in), custom_call_target="tpu_custom_call" | custom-call | tf_op jit(solution)/shard_map/pallas_call | solution.py:481

commit v4 on v3

--- a/solution.py
+++ b/solution.py
@@ -155,8 +155,6 @@
         some = ref.at[pl.ds(0, rows)]
         pltpu.make_async_copy(some, some, sem.at[stage, wave, c * 3 + r]).wait()
 
-    for copy in token_copies:
-        copy.wait()
     seqs, heads, latent = ql_v.shape
     rope = cr_v.shape[1]
     cached = cr_v.shape[2]
@@ -189,14 +187,14 @@
 
     pl.semaphore_wait(barrier, 1 + 3 * 3 * 2)
 
-    def send_own(stage, axis, refs, c, r):
+    def send_own(stage, axis, src, refs, c, r):
         along = ROTATIONS[r][axis]
         block = refs.at[parity, own_slot(r)]
         for k in (1, 3, 2):
-            remote(block, block, stage, parity, c, r, device(**{along: (me[along] + k) % SIDE})).start()
+            remote(src, block, stage, parity, c, r, device(**{along: (me[along] + k) % SIDE})).start()
 
     for c, r in PARTS:
-        send_own(GATHER_A, 0, held[c][r], c, r)
+        send_own(GATHER_A, 0, tokens.at[:, pl.ds(*COLS[c][r])], held[c][r], c, r)
 
     for copy in small:
         copy.wait()
@@ -218,12 +216,12 @@
         codes_v[r][parity, own_slot(r), :] = code
 
     for c, r in PARTS:
-        send_own(GATHER_B, 1, held[c][r], c, r)
+        send_own(GATHER_B, 1, tokens.at[:, pl.ds(*COLS[c][r])], held[c][r], c, r)
     for r in range(3):
-        send_own(CODE_A, 0, codes_v[r], 0, r)
+        send_own(CODE_A, 0, codes_v[r].at[parity, own_slot(r)], codes_v[r], 0, r)
     for r in range(3):
-        send_own(CODE_B, 1, codes_v[r], 0, r)
-    for copy in attention_copies:
+        send_own(CODE_B, 1, codes_v[r].at[parity, own_slot(r)], codes_v[r], 0, r)
+    for copy in token_copies + attention_copies:
         copy.wait()
     for copy in weight_copies:
         copy.start()

time: 53.4 us -> 53.6 us (level)
  no operation moved by 1% of the time
where the time goes in v4:
time: 53.6 us; the launch traced here: 53.4 us
  Pallas kernels  52.8 us (99%)
  between operations  0.64 us (1%)
    pallas_call x1, Pallas kernels, per_device(): pl.pallas_call(kernel, out_shape=(jax.ShapeDtypeStruct((tok_dev, width),...  50.9 us
    pallas_call x1, Pallas kernels, per_device(): pl.pallas_call(finish, out_shape=tuple((jax.ShapeDtypeStruct(x.shape, x.d...  1.85 us

profile of v4, /device:TPU:2, one launch (start us, length us, event | category | flops | bytes accessed | tf_op | source)
XLA Modules:
  0.0 53.4 jit_solution(7440157256864316680)
XLA Ops:
  0.6 50.9 %shard_map.122 = (bf16[16,3584]{1,0:T(8,128)(2,1)}, bf16[8,32768]{1,0:T(8,128)(2,1)}) custom-call(bf16[16,3584]{1,0:T(8,128)(2,1)} %tokens.1, s32[8,16]{1,0:T(8,128)} %bitcast.2, f32[8,16]{1,0:T(8,128)} %bitcast.3, bf16[1,3584,1024]{2,1,0:T(8,128)(2,1)} %w_gate.1, bf16[1,3584,1024]{2,1,0:T(8,128)(2,1)} %w_up.1, bf16[1,1024,3584]{2,1,0:T(8,128)(2,1)} %w_down.1, ...), custom_call_target="tpu_custom_call" | custom-call | tf_op jit(solution)/shard_map/pallas_call | solution.py:465
  51.6 1.9 %shard_map.123 = (bf16[16,3584]{1,0:T(8,128)(2,1)}, bf16[8,32768]{1,0:T(8,128)(2,1)}) custom-call(bf16[16,3584]{1,0:T(8,128)(2,1)} %get-tuple-element.4.moe_in, bf16[8,32768]{1,0:T(8,128)(2,1)} %get-tuple-element.5.attn_in), custom_call_target="tpu_custom_call" | custom-call | tf_op jit(solution)/shard_map/pallas_call | solution.py:479

commit v5 on v4

--- a/solution.py
+++ b/solution.py
@@ -346,11 +346,12 @@
             return 0
 
         lax.fori_loop(0, ff // step, ff_tile, 0, unroll=True)
-        hidden_r[...] = lax.dot_general(
-            perm[wave], hidden[...], (((0,), (0,)), ((), ())), preferred_element_type=F32
-        ).astype(BF16)
         for c, r in PARTS:
             start, width = COLS[c][r]
+            if r == 1 and c == 0:
+                hidden_r[...] = lax.dot_general(
+                    perm[wave], hidden[...], (((0,), (0,)), ((), ())), preferred_element_type=F32
+                ).astype(BF16)
             rows = hidden[...] if r == 0 else hidden_r[pl.ds((r - 1) * ROWS, ROWS), :]
             result[wave][c][r][...] = dot(rows, down_v[:, pl.ds(start, width)]).astype(BF16)
             exchange(result[wave][c][r], back[wave][c][r], FROM_EXPERT, wave, c, r)

time: 53.6 us -> 53.5 us (level)
  no operation moved by 1% of the time
where the time goes in v5:
time: 53.5 us; the launch traced here: 53.4 us
  Pallas kernels  52.8 us (99%)
  between operations  0.64 us (1%)
    pallas_call x1, Pallas kernels, per_device(): pl.pallas_call(kernel, out_shape=(jax.ShapeDtypeStruct((tok_dev, width),...  50.9 us
    pallas_call x1, Pallas kernels, per_device(): pl.pallas_call(finish, out_shape=tuple((jax.ShapeDtypeStruct(x.shape, x.d...  1.85 us

profile of v5, /device:TPU:2, one launch (start us, length us, event | category | flops | bytes accessed | tf_op | source)
XLA Modules:
  0.0 53.4 jit_solution(7345052784876965373)
XLA Ops:
  0.6 50.9 %shard_map.122 = (bf16[16,3584]{1,0:T(8,128)(2,1)}, bf16[8,32768]{1,0:T(8,128)(2,1)}) custom-call(bf16[16,3584]{1,0:T(8,128)(2,1)} %tokens.1, s32[8,16]{1,0:T(8,128)} %bitcast.2, f32[8,16]{1,0:T(8,128)} %bitcast.3, bf16[1,3584,1024]{2,1,0:T(8,128)(2,1)} %w_gate.1, bf16[1,3584,1024]{2,1,0:T(8,128)(2,1)} %w_up.1, bf16[1,1024,3584]{2,1,0:T(8,128)(2,1)} %w_down.1, ...), custom_call_target="tpu_custom_call" | custom-call | tf_op jit(solution)/shard_map/pallas_call | solution.py:466
  51.6 1.9 %shard_map.123 = (bf16[16,3584]{1,0:T(8,128)(2,1)}, bf16[8,32768]{1,0:T(8,128)(2,1)}) custom-call(bf16[16,3584]{1,0:T(8,128)(2,1)} %get-tuple-element.4.moe_in, bf16[8,32768]{1,0:T(8,128)(2,1)} %get-tuple-element.5.attn_in), custom_call_target="tpu_custom_call" | custom-call | tf_op jit(solution)/shard_map/pallas_call | solution.py:480
